TPU v7x, 32 devices: a whole 2x2x4 slice. The times are simulated.
32 devices in a mesh: sub: 16 (over z, y, core), rng: 2 (over x).
Axes of the slice: x: 2, y: 2, z: 4, core: 2. Of those that a mesh axis runs over, the one named last changes fastest.
Arguments:
- polar_image: float32 [2, 16, 256, 2048], P(None, 'sub', None, 'rng'), may hold values from -6 to 6
- beam_tap: int32 [3, 2, 512], replicated, may hold values from 0 to 254, as said below
- beam_frac: float32 [3, 2, 512], replicated, may hold values from 0 to 1
- range_shift: int32 [3, 2, 512], replicated, may hold values from -24 to 24
- range_weight: float32 [3, 2, 4, 512], replicated, may hold values from 0.05 to 0.45
- phase_rate: float32 [3, 2, 512], replicated, may hold values from -16 to 16
- phase_offset: float32 [3, 2, 512], replicated, may hold values from -0.5 to 0.5
Outputs:
- merged: float32 [2, 16, 256, 2048], P(None, 'sub', None, 'rng')
Inputs may be any that keep to these rules, and one draw needn't show every extreme that they name: For output position p, beam_tap and beam_tap + 1 lie in the aligned group of child beams 4 (p // 8) to 4 (p // 8) + 3.
All inputs are finite; a program needn't handle non-finite values.
Results may differ from a plain program's by a relative error of at most 0.0003.
Values sent between devices are 32-bit elements; how exact they have to be, the bound alone decides.
A program may use at most 64 MiB of HBM per device.

v0:
```python
import functools
import math

import jax
import jax.numpy as jnp
from jax import lax
from jax.experimental import pallas as pl
from jax.experimental.pallas import tpu as pltpu
from jax.sharding import PartitionSpec as P

SECTIONS = 3
SHIFT = 24
WAYS = 2**SECTIONS
TAPS = 4
LANES = 128
MOVES = (43, 43, 42)
FIELDS = 16
MESH = pl.DeviceIdType.MESH
WEIGHT, BLEND, FIRST, COS, SIN, STEP_COS, STEP_SIN, PLANES = 0, 4, 8, 9, 10, 11, 12, 13


def flipped(place, mask):
    for bit in range(SECTIONS):
        if mask >> bit & 1:
            place = place + (1 << bit) * (1 - 2 * (place // (1 << bit) % 2))
    return place


def cos_sin(cycles):
    half = (cycles - jnp.round(cycles)) * math.pi
    sq = half * half
    s = jnp.full_like(half, -1.0 / math.factorial(11))
    for n in (9, 7, 5, 3, 1):
        s = s * sq + (1.0 if n % 4 == 1 else -1.0) / math.factorial(n)
    s = s * half
    c = jnp.full_like(half, 1.0 / math.factorial(12))
    for n in (10, 8, 6, 4, 2, 0):
        c = c * sq + (1.0 if n % 4 == 0 else -1.0) / math.factorial(n)
    return 1.0 - 2.0 * s * s, 2.0 * s * c


def lane_take(x, idx):
    return jnp.take_along_axis(x, idx, axis=1, mode="promise_in_bounds")


def kernel(
    group_step, chunk, span,
    img, tap, frac, shift, wgt, rate, off, out,
    x0, x1, x2, x3, tmp, tab, coef,
    send_sem, recv_sem, own_sem, halo_send, halo_recv, out_sem,
):
    me, col = lax.axis_index("sub"), lax.axis_index("rng")
    place, inner = me // group_step, me % group_step
    row_len = img.shape[3]
    eighth = x0.shape[2]
    chunks = eighth // chunk
    width = x0.shape[3]
    blocks = width // LANES
    other = 1 - col
    col_base = col * (row_len - LANES)
    own_at = pl.multiple_of(col * LANES, LANES)

    def sub_of(p):
        return p * group_step + inner

    barrier = pltpu.get_barrier_semaphore()
    for x in range(1, WAYS):
        pl.semaphore_signal(barrier, inc=1, device_id=(sub_of(flipped(place, x)), col), device_id_type=MESH)
    pl.semaphore_signal(barrier, inc=1, device_id=(me, other), device_id_type=MESH)

    def own_copy(c):
        return pltpu.make_async_copy(
            img.at[:, 0, pl.ds(pl.multiple_of(place * eighth + c * chunk, 8), chunk), :],
            x0.at[:, place, pl.ds(c * chunk, chunk), pl.ds(own_at, row_len)],
            own_sem.at[c],
        )

    def piece(c, x, sending):
        peer = flipped(place, x)
        row = place if sending else peer
        return pltpu.make_async_remote_copy(
            src_ref=img.at[:, 0, pl.ds(pl.multiple_of(peer * eighth + c * chunk, 8), chunk), :],
            dst_ref=x0.at[:, row, pl.ds(c * chunk, chunk), pl.ds(own_at, row_len)],
            send_sem=send_sem.at[c, x],
            recv_sem=recv_sem.at[c, x],
            device_id=(sub_of(peer), col),
            device_id_type=MESH,
        )

    def halo(c, sending):
        src = pl.multiple_of((1 - col) * (row_len - LANES) + col * LANES, LANES)
        who = col if sending else other
        dst = pl.multiple_of(who * row_len, LANES)
        return pltpu.make_async_remote_copy(
            src_ref=x0.at[:, :, pl.ds(c * chunk, chunk), pl.ds(src, LANES)],
            dst_ref=x0.at[:, :, pl.ds(c * chunk, chunk), pl.ds(dst, LANES)],
            send_sem=halo_send.at[c],
            recv_sem=halo_recv.at[c],
            device_id=(me, other),
            device_id_type=MESH,
        )

    for c in range(chunks):
        own_copy(c).start()
    pl.semaphore_wait(barrier, WAYS)
    order = (4, 5, 6, 7, 2, 3, 1)
    for c in range(chunks):
        for x in order:
            piece(c, x, True).start()

    tmp[...] = jnp.zeros_like(tmp)
    for k in range(SECTIONS):
        for j in range(2):
            base = (k * 2 + j) * FIELDS
            tmp[base : base + 1, :] = tap[k, j : j + 1, :].astype(jnp.float32)
            tmp[base + 1 : base + 2, :] = frac[k, j : j + 1, :]
            tmp[base + 2 : base + 3, :] = shift[k, j : j + 1, :].astype(jnp.float32)
            tmp[base + 3 : base + 7, :] = wgt[k, j]
            tmp[base + 7 : base + 8, :] = rate[k, j : j + 1, :]
            tmp[base + 8 : base + 9, :] = off[k, j : j + 1, :]
    for n in range(tab.shape[0] // LANES):
        tab[n * LANES : (n + 1) * LANES, :] = tmp[:, n * LANES : (n + 1) * LANES].T
    lane = lax.broadcasted_iota(jnp.int32, (8, LANES), 1)

    at = []
    first_group = 0
    moved = LANES
    for k in range(SECTIONS):
        in_beams = eighth << k
        remaining = place % (1 << (SECTIONS - k))
        in_start = remaining * in_beams
        groups = in_beams // 4
        moved -= MOVES[k]
        at.append((first_group, groups, moved))

        def plan(g, carry, k=k, in_start=in_start, groups=groups, first=first_group, moved=moved):
            rows = tab[pl.ds(pl.multiple_of(2 * in_start + 8 * g, 8), 8), :]
            for j in range(2):
                def field(q):
                    n = (k * 2 + j) * FIELDS + q
                    return jnp.broadcast_to(rows[:, n : n + 1], (8, LANES))
                to = first + j * groups + g
                local = field(0) - (in_start + 4 * g).astype(jnp.float32)
                f = field(1)
                for b in range(4):
                    coef[to, BLEND + b] = jnp.where(local == b, 1.0 - f, 0.0) + jnp.where(local == b - 1, f, 0.0)
                coef[to, FIRST] = field(2) + float(SHIFT + MOVES[k] - SHIFT - 1)
                for t in range(TAPS):
                    coef[to, WEIGHT + t] = field(3 + t)
                r = (lane - moved + col_base).astype(jnp.float32) + 0.5
                cyc = field(7)
                c0, s0 = cos_sin(cyc * (r / span) + field(8))
                c1, s1 = cos_sin(cyc * (LANES / span))
                coef[to, COS] = c0
                coef[to, SIN] = s0
                coef[to, STEP_COS] = c1
                coef[to, STEP_SIN] = s1
            return carry

        lax.fori_loop(0, groups, plan, 0)
        first_group += 2 * groups

    def merge(k, src, dst, row, rows, g, half):
        first, groups, left = at[k]
        count = blocks + 1 if k < SECTIONS - 1 else blocks
        grp = 2 * g + half
        for j in range(2):
            to = first + j * groups + grp
            d0 = coef[to, FIRST].astype(jnp.int32)
            idx = [(lane + (d0 + t)) & (LANES - 1) for t in range(TAPS)]
            nxt = [lane < d0 + t for t in range(TAPS)]
            w = [coef[to, WEIGHT + t] for t in range(TAPS)]
            bl = [coef[to, BLEND + b] for b in range(4)]
            pc, ps = coef[to, COS], coef[to, SIN]
            sc, ss = coef[to, STEP_COS], coef[to, STEP_SIN]

            def angled(ch, block):
                block = block - 1 if k == 0 else block
                if block < 0 or (block + 1) * LANES > src.shape[3]:
                    return jnp.zeros((8, LANES), jnp.float32)
                tile = src[ch, rows[j], pl.ds(pl.multiple_of(8 * g, 8), 8), block * LANES : (block + 1) * LANES]
                total = None
                for b in range(4):
                    term = bl[b] * jnp.broadcast_to(tile[4 * half + b : 4 * half + b + 1, :], (8, LANES))
                    total = term if total is None else total + term
                return total

            cur = [angled(ch, 0) for ch in range(2)]
            for block in range(count):
                ahead = [angled(ch, block + 1) for ch in range(2)]
                ranged = []
                for ch in range(2):
                    total = None
                    for t in range(TAPS):
                        term = w[t] * lane_take(jnp.where(nxt[t], ahead[ch], cur[ch]), idx[t])
                        total = term if total is None else total + term
                    ranged.append(total)
                re = ranged[0] * pc - ranged[1] * ps
                im = ranged[0] * ps + ranged[1] * pc
                place_at = (pl.ds(pl.multiple_of(8 * grp, 8), 8), slice(block * LANES, (block + 1) * LANES))
                if j == 1:
                    re = re + dst[0, row, place_at[0], place_at[1]]
                    im = im + dst[1, row, place_at[0], place_at[1]]
                    if k < SECTIONS - 1 and block in (0, count - 1):
                        r = lane + (block * LANES - left + col_base)
                        inside = (r >= 0) & (r < span)
                        re = jnp.where(inside, re, 0.0)
                        im = jnp.where(inside, im, 0.0)
                dst[0, row, place_at[0], place_at[1]] = re
                dst[1, row, place_at[0], place_at[1]] = im
                if block < count - 1:
                    pc, ps = pc * sc - ps * ss, pc * ss + ps * sc
                cur = ahead

    def out_copy(c):
        n = chunk * WAYS
        return pltpu.make_async_copy(
            x3.at[:, 0, pl.ds(c * n, n), pl.ds(own_at, row_len)],
            out.at[:, 0, pl.ds(c * n, n), :],
            out_sem.at[c],
        )

    def compute(c):
        buffers = (x0, x1, x2, x3)
        for k in range(SECTIONS):
            n_rows = WAYS >> (k + 1)
            pairs = (chunk << k) // 8

            def body(it, carry, k=k, n_rows=n_rows, pairs=pairs):
                row, g = it // pairs, it % pairs
                for half in range(2):
                    merge(k, buffers[k], buffers[k + 1], row, (row, row + n_rows), c * pairs + g, half)
                return carry

            lax.fori_loop(0, n_rows * pairs, body, 0)
        out_copy(c).start()

    def arrive(c):
        own_copy(c).wait()
        for x in order:
            piece(c, x, False).wait_recv()
        halo(c, True).start()

    arrive(0)
    for c in range(chunks):
        if c + 1 < chunks:
            halo(c, False).wait_recv()
            compute(c)
            arrive(c + 1)
        else:
            halo(c, False).wait_recv()
            compute(c)
    for c in range(chunks):
        for x in order:
            piece(c, x, True).wait_send()
        halo(c, True).wait_send()
        out_copy(c).wait()


def on_device(polar_image, beam_tap, beam_frac, range_shift, range_weight, phase_rate, phase_offset):
    _, sub_count, beams, row_len = polar_image.shape
    eighth = beams // WAYS
    chunk = 8
    chunks = eighth // chunk
    group_step = lax.axis_size("sub") // WAYS
    width = row_len + LANES
    positions = beam_tap.shape[2]
    vmem = pl.BlockSpec(memory_space=pltpu.VMEM)
    hbm = pl.BlockSpec(memory_space=pl.ANY)
    n_groups = sum(2 * ((eighth << k) // 4) for k in range(SECTIONS))
    return pl.pallas_call(
        functools.partial(kernel, group_step, chunk, row_len * lax.axis_size("rng")),
        out_shape=jax.ShapeDtypeStruct(polar_image.shape, jnp.float32),
        in_specs=[hbm] + [vmem] * 6,
        out_specs=hbm,
        scratch_shapes=[
            pltpu.VMEM((2, WAYS, eighth, width), jnp.float32),
            pltpu.VMEM((2, WAYS // 2, 2 * eighth, width + LANES), jnp.float32),
            pltpu.VMEM((2, WAYS // 4, 4 * eighth, width + LANES), jnp.float32),
            pltpu.VMEM((2, 1, beams, width), jnp.float32),
            pltpu.VMEM((LANES, positions), jnp.float32),
            pltpu.VMEM((positions, LANES), jnp.float32),
            pltpu.VMEM((n_groups, PLANES, 8, LANES), jnp.float32),
            pltpu.SemaphoreType.DMA((chunks, WAYS)),
            pltpu.SemaphoreType.DMA((chunks, WAYS)),
            pltpu.SemaphoreType.DMA((chunks,)),
            pltpu.SemaphoreType.DMA((chunks,)),
            pltpu.SemaphoreType.DMA((chunks,)),
            pltpu.SemaphoreType.DMA((chunks,)),
        ],
        compiler_params=pltpu.CompilerParams(
            collective_id=0, has_side_effects=True, vmem_limit_bytes=48 * 2**20
        ),
    )(polar_image, beam_tap, beam_frac, range_shift, range_weight, phase_rate, phase_offset)


def solution(mesh):
    placed = (P(None, "sub", None, "rng"), P(), P(), P(), P(), P(), P())
    return jax.shard_map(
        on_device,
        mesh=mesh,
        in_specs=placed,
        out_specs=P(None, "sub", None, "rng"),
        check_vma=False,
    )
```

profile of v0, /device:TPU:16, one launch (start us, length us, event | category | flops | bytes accessed | tf_op | source)
XLA Modules:
  0.0 91.0 jit_solution(13955807364198185088)
XLA Ops:
  0.0 0.0 copy-start
  0.0 1.6 %copy-done = f32[2,1,256,1024]{3,2,1,0:T(8,128)S(1)} copy-done((f32[2,1,256,1024]{3,2,1,0:T(8,128)S(1)}, f32[2,1,256,1024]{3,2,1,0:T(8,128)}, u32[]{:S(2)}) %copy-start) | copy-done | bytes 2097176
  1.6 0.0 copy-start.1
  1.6 0.8 copy-done.1
  2.4 0.0 copy-start.2
  2.4 0.7 copy-done.2
  3.1 0.0 copy-start.3
  3.1 0.7 copy-done.3
  3.8 0.0 copy-start.4
  3.8 0.7 copy-done.4
  4.5 0.0 copy-start.5
  4.5 0.7 copy-done.5
  5.2 0.0 copy-start.6
  5.2 0.7 copy-done.6
  5.9 83.7 %shard_map.73 = f32[2,1,256,1024]{3,2,1,0:T(8,128)S(1)} custom-call(f32[2,1,256,1024]{3,2,1,0:T(8,128)S(1)} %copy-done, s32[3,2,512]{2,1,0:T(2,128)S(1)} %copy-done.2, f32[3,2,512]{2,1,0:T(2,128)S(1)} %copy-done.3, s32[3,2,512]{2,1,0:T(2,128)S(1)} %copy-done.4, f32[3,2,4,512]{3,2,1,0:T(4,128)S(1)} %copy-done.1, f32[3,2,512]{2,1,0:T(2,128)S(1)} %copy-done.5, ...), custom_call_target="tpu_custom_call" | custom-call | tf_op jit(solution)/shard_map/pallas_call | solution.py:271
  89.7 1.3 %copy.9 = f32[2,1,256,1024]{3,2,1,0:T(8,128)} copy(f32[2,1,256,1024]{3,2,1,0:T(8,128)S(1)} %shard_map.73) | data formatting | bytes 4194304
Async XLA Ops:
  0.0 1.6 %copy-start = (f32[2,1,256,1024]{3,2,1,0:T(8,128)S(1)}, f32[2,1,256,1024]{3,2,1,0:T(8,128)}, u32[]{:S(2)}) copy-start(f32[2,1,256,1024]{3,2,1,0:T(8,128)} %img.1) | copy-start | bytes 6291460
  1.6 0.8 copy-start.1
  2.4 0.7 copy-start.2
  3.1 0.7 copy-start.3
  3.8 0.7 copy-start.4
  4.5 0.7 copy-start.5
  5.2 0.7 copy-start.6
where the time goes:
time: 91.5 us; the launch traced here: 91 us
  Pallas kernels  83.7 us (91%)
  local copies, waits for them, and re-layouts  7.24 us (8%)
    pallas_call x1, Pallas kernels, on_device(): pl.pallas_call(functools.partial(kernel, group_step, chunk, row_len * lax...  83.7 us
    unnamed x15, local copies, waits for them, and re-layouts  7.24 us

commit v1 on v0

--- a/solution.py
+++ b/solution.py
@@ -45,9 +45,10 @@
 
 def kernel(
     group_step, chunk, span,
-    img, tap, frac, shift, wgt, rate, off, out,
+    img, tap_in, frac_in, shift_in, wgt_in, rate_in, off_in, out,
+    tap, frac, shift, wgt, rate, off,
     x0, x1, x2, x3, tmp, tab, coef,
-    send_sem, recv_sem, own_sem, halo_send, halo_recv, out_sem,
+    table_sem, send_sem, recv_sem, own_sem, halo_send, halo_recv, out_sem,
 ):
     me, col = lax.axis_index("sub"), lax.axis_index("rng")
     place, inner = me // group_step, me % group_step
@@ -100,13 +101,22 @@
             device_id_type=MESH,
         )
 
-    for c in range(chunks):
-        own_copy(c).start()
+    tables = [
+        pltpu.make_async_copy(a, b, table_sem.at[n])
+        for n, (a, b) in enumerate(
+            zip((tap_in, frac_in, shift_in, wgt_in, rate_in, off_in), (tap, frac, shift, wgt, rate, off))
+        )
+    ]
+    for copy in tables:
+        copy.start()
     pl.semaphore_wait(barrier, WAYS)
     order = (4, 5, 6, 7, 2, 3, 1)
     for c in range(chunks):
         for x in order:
             piece(c, x, True).start()
+        own_copy(c).start()
+    for copy in tables:
+        copy.wait()
 
     tmp[...] = jnp.zeros_like(tmp)
     for k in range(SECTIONS):
@@ -164,11 +174,11 @@
         first, groups, left = at[k]
         count = blocks + 1 if k < SECTIONS - 1 else blocks
         grp = 2 * g + half
+        results = []
         for j in range(2):
             to = first + j * groups + grp
             d0 = coef[to, FIRST].astype(jnp.int32)
-            idx = [(lane + (d0 + t)) & (LANES - 1) for t in range(TAPS)]
-            nxt = [lane < d0 + t for t in range(TAPS)]
+            idx, nxt = (lane + d0) & (LANES - 1), lane < d0
             w = [coef[to, WEIGHT + t] for t in range(TAPS)]
             bl = [coef[to, BLEND + b] for b in range(4)]
             pc, ps = coef[to, COS], coef[to, SIN]
@@ -185,32 +195,37 @@
                     total = term if total is None else total + term
                 return total
 
-            cur = [angled(ch, 0) for ch in range(2)]
+            def shifted(now, then):
+                return [lane_take(jnp.where(nxt, b, a), idx) for a, b in zip(now, then)]
+
+            def ahead_by(n, now, then):
+                return pltpu.roll(jnp.where(lane < n, then, now), LANES - n, axis=1)
+
+            def taps(now, then):
+                pairs = [(a, ahead_by(1, a, b)) for a, b in zip(now, then)]
+                return [w[0] * a + w[1] * b for a, b in pairs], [w[2] * a + w[3] * b for a, b in pairs]
+
+            angles = [[angled(ch, n) for ch in range(2)] for n in range(blocks + 2)]
+            shifts = [shifted(angles[n], angles[n + 1]) for n in range(blocks + 1)]
+            made = [taps(shifts[n], shifts[min(n + 1, blocks)]) for n in range(blocks + 1)]
             for block in range(count):
-                ahead = [angled(ch, block + 1) for ch in range(2)]
-                ranged = []
-                for ch in range(2):
-                    total = None
-                    for t in range(TAPS):
-                        term = w[t] * lane_take(jnp.where(nxt[t], ahead[ch], cur[ch]), idx[t])
-                        total = term if total is None else total + term
-                    ranged.append(total)
+                now, then = made[block], made[min(block + 1, blocks)]
+                ranged = [now[0][ch] + ahead_by(2, now[1][ch], then[1][ch]) for ch in range(2)]
                 re = ranged[0] * pc - ranged[1] * ps
                 im = ranged[0] * ps + ranged[1] * pc
-                place_at = (pl.ds(pl.multiple_of(8 * grp, 8), 8), slice(block * LANES, (block + 1) * LANES))
-                if j == 1:
-                    re = re + dst[0, row, place_at[0], place_at[1]]
-                    im = im + dst[1, row, place_at[0], place_at[1]]
-                    if k < SECTIONS - 1 and block in (0, count - 1):
-                        r = lane + (block * LANES - left + col_base)
-                        inside = (r >= 0) & (r < span)
-                        re = jnp.where(inside, re, 0.0)
-                        im = jnp.where(inside, im, 0.0)
-                dst[0, row, place_at[0], place_at[1]] = re
-                dst[1, row, place_at[0], place_at[1]] = im
+                if j == 0:
+                    results.append((re, im))
+                else:
+                    results[block] = (results[block][0] + re, results[block][1] + im)
                 if block < count - 1:
                     pc, ps = pc * sc - ps * ss, pc * ss + ps * sc
-                cur = ahead
+        for block, pair in enumerate(results):
+            if k < SECTIONS - 1 and block in (0, count - 1):
+                r = lane + (block * LANES - left + col_base)
+                pair = [jnp.where((r >= 0) & (r < span), part, 0.0) for part in pair]
+            for ch in range(2):
+                at_rows = pl.ds(pl.multiple_of(8 * grp, 8), 8)
+                dst[ch, row, at_rows, block * LANES : (block + 1) * LANES] = pair[ch]
 
     def out_copy(c):
         n = chunk * WAYS
@@ -258,6 +273,7 @@
 
 
 def on_device(polar_image, beam_tap, beam_frac, range_shift, range_weight, phase_rate, phase_offset):
+    tables = (beam_tap, beam_frac, range_shift, range_weight, phase_rate, phase_offset)
     _, sub_count, beams, row_len = polar_image.shape
     eighth = beams // WAYS
     chunk = 8
@@ -265,15 +281,15 @@
     group_step = lax.axis_size("sub") // WAYS
     width = row_len + LANES
     positions = beam_tap.shape[2]
-    vmem = pl.BlockSpec(memory_space=pltpu.VMEM)
     hbm = pl.BlockSpec(memory_space=pl.ANY)
     n_groups = sum(2 * ((eighth << k) // 4) for k in range(SECTIONS))
     return pl.pallas_call(
         functools.partial(kernel, group_step, chunk, row_len * lax.axis_size("rng")),
         out_shape=jax.ShapeDtypeStruct(polar_image.shape, jnp.float32),
-        in_specs=[hbm] + [vmem] * 6,
+        in_specs=[hbm] * 7,
         out_specs=hbm,
-        scratch_shapes=[
+        scratch_shapes=[pltpu.VMEM(a.shape, a.dtype) for a in tables]
+        + [
             pltpu.VMEM((2, WAYS, eighth, width), jnp.float32),
             pltpu.VMEM((2, WAYS // 2, 2 * eighth, width + LANES), jnp.float32),
             pltpu.VMEM((2, WAYS // 4, 4 * eighth, width + LANES), jnp.float32),
@@ -281,6 +297,7 @@
             pltpu.VMEM((LANES, positions), jnp.float32),
             pltpu.VMEM((positions, LANES), jnp.float32),
             pltpu.VMEM((n_groups, PLANES, 8, LANES), jnp.float32),
+            pltpu.SemaphoreType.DMA((len(tables),)),
             pltpu.SemaphoreType.DMA((chunks, WAYS)),
             pltpu.SemaphoreType.DMA((chunks, WAYS)),
             pltpu.SemaphoreType.DMA((chunks,)),
@@ -289,9 +306,9 @@
             pltpu.SemaphoreType.DMA((chunks,)),
         ],
         compiler_params=pltpu.CompilerParams(
-            collective_id=0, has_side_effects=True, vmem_limit_bytes=48 * 2**20
+            collective_id=0, has_side_effects=True, vmem_limit_bytes=60 * 2**20
         ),
-    )(polar_image, beam_tap, beam_frac, range_shift, range_weight, phase_rate, phase_offset)
+    )(polar_image, *tables)
 
 
 def solution(mesh):

time: 91.5 us -> 74 us (0.81)
  Pallas kernels: 83.7 us -> 70.7 us
  local copies, waits for them, and re-layouts: 7.24 us -> 3.16 us
    pallas_call x1, Pallas kernels: 83.7 us -> 70.7 us  [on_device(): pl.pallas_call(functools.partial(kernel, group_step, chunk, row_len * lax...]
    unnamed x15 -> x1, local copies, waits for them, and re-layouts: 7.24 us -> 3.16 us
where the time goes in v1:
time: 74 us; the launch traced here: 73.9 us
  Pallas kernels  70.7 us (96%)
  local copies, waits for them, and re-layouts  3.16 us (4%)
    pallas_call x1, Pallas kernels, on_device(): pl.pallas_call(functools.partial(kernel, group_step, chunk, row_len * lax...  70.7 us
    unnamed x1, local copies, waits for them, and re-layouts  3.16 us

profile of v1, /device:TPU:16, one launch (start us, length us, event | category | flops | bytes accessed | tf_op | source)
XLA Modules:
  0.0 73.9 jit_solution(10199722070801440126)
XLA Ops:
  0.0 70.7 %shard_map.73 = f32[2,1,256,1024]{3,2,1,0:T(8,128)} custom-call(f32[2,1,256,1024]{3,2,1,0:T(8,128)} %img.1, s32[3,2,512]{2,1,0:T(2,128)} %tap_in.1, f32[3,2,512]{2,1,0:T(2,128)} %frac_in.1, s32[3,2,512]{2,1,0:T(2,128)} %shift_in.1, f32[3,2,4,512]{3,2,1,0:T(4,128)} %wgt_in.1, f32[3,2,512]{2,1,0:T(2,128)} %rate_in.1, f32[3,2,512]{2,1,0:T(2,128)} %off_in.1), custom_call_target="tpu_custom_call" | custom-call | tf_op jit(solution)/shard_map/pallas_call | solution.py:286
  70.7 3.2 %copy.9 = f32[2,1,256,1024]{3,2,1,0:T(8,128)} copy(f32[2,1,256,1024]{3,2,1,0:T(8,128)} %shard_map.73) | data formatting | bytes 4194304
